TPU v7x, 512 devices: a whole 4x8x8 slice. The times are simulated.
512 devices in a mesh: clip: 32 (over x, z), seq: 16 (over y, core).
Axes of the slice: x: 4, y: 8, z: 8, core: 2. Of those that a mesh axis runs over, the one named last changes fastest.
Arguments:
- queries: bfloat16 [65536, 4096], P(('clip', 'seq')), parts along dimension 0, may hold values from -8 to 8
- keys_in: bfloat16 [65536, 4096], P(('clip', 'seq')), parts along dimension 0, may hold values from -8 to 8
- value_input: bfloat16 [65536, 4096], P(('clip', 'seq')), parts along dimension 0, may hold values from -6 to 6
- head_class: int32 [1024], P('clip'), parts along dimension 0, may hold values from 0 to 1, as said below
- block_lists: int32 [1024, 16, 4], P('clip'), parts along dimension 0, may hold values from 0 to 15, as said below
Outputs:
- attended: bfloat16 [65536, 4096], P(('clip', 'seq')), parts along dimension 0
There are 32 independent parts, one for each index of `clip`. A program takes and returns all parts, laid end to end along the dimension named above; each array names one. Nothing has to cross between parts.
Inputs may be any that keep to these rules, and one draw needn't show every extreme that they name: `head_class`: exactly 8 heads have class 1. Each row block_lists[h, i, :] holds 4 different block numbers, one of them i itself.
All inputs are finite; a program needn't handle non-finite values.
Results may differ from a plain program's by a relative error of at most 0.0046.
Values may be sent and summed in bfloat16 or wider, within the bound.
A program may use at most 64 MiB of HBM per device.

v0:
```python
import math

import jax
import jax.numpy as jnp
from jax import lax
from jax.sharding import PartitionSpec as P

BLOCK_LEN = 128


def soft_block(scores):
    largest = jnp.max(scores, axis=-1, keepdims=True)
    weights = jnp.exp(scores - largest)
    total = jnp.sum(weights, axis=-1, keepdims=True)
    return (weights.astype(jnp.bfloat16), total)


def dense_head(query_head_slice, key_head, value_head, head_lists):
    length = query_head_slice.shape[0]
    head_dim = query_head_slice.shape[1]
    scale = 1.0 / math.sqrt(head_dim)
    row_block = min(512, length)
    stacked = query_head_slice.reshape(length // row_block, row_block, head_dim)

    def attend_rows(query_rows):
        scores = jnp.dot(query_rows, key_head.T, preferred_element_type=jnp.float32) * scale
        rounded_result, total = soft_block(scores)
        mixed = jnp.dot(rounded_result, value_head, preferred_element_type=jnp.float32) / total
        return mixed.astype(jnp.bfloat16)

    return lax.map(attend_rows, stacked).reshape(length, head_dim)


def sparse_head(query_head_slice, key_head, value_head, head_lists):
    length = query_head_slice.shape[0]
    head_dim = query_head_slice.shape[1]
    scale = 1.0 / math.sqrt(head_dim)
    block_count = length // BLOCK_LEN
    query_block_tiles = query_head_slice.reshape(block_count, BLOCK_LEN, head_dim)
    key_block_tiles = jnp.take(
        key_head.reshape(block_count, BLOCK_LEN, head_dim), head_lists, axis=0
    )
    value_block_tiles = jnp.take(
        value_head.reshape(block_count, BLOCK_LEN, head_dim), head_lists, axis=0
    )
    key_block_tiles = key_block_tiles.reshape(block_count, -1, head_dim)
    value_block_tiles = value_block_tiles.reshape(block_count, -1, head_dim)
    scores = (
        jnp.einsum(
            "oui,ofi->ouf", query_block_tiles, key_block_tiles, preferred_element_type=jnp.float32
        )
        * scale
    )
    rounded_result, total = soft_block(scores)
    mixed = (
        jnp.einsum(
            "xln,xnc->xlc", rounded_result, value_block_tiles, preferred_element_type=jnp.float32
        )
        / total
    )
    return mixed.astype(jnp.bfloat16).reshape(length, head_dim)


def local(queries, keys_in, value_input, head_class, block_lists):
    group = lax.axis_size("seq")
    tok_rows = queries.shape[0]
    heads_all = head_class.shape[0]
    head_dim = queries.shape[1] // heads_all
    per_device = heads_all // group
    positions = jnp.arange(heads_all, dtype=jnp.int32)
    shaped_q = queries.reshape(tok_rows, heads_all, head_dim)
    shaped_k = keys_in.reshape(tok_rows, heads_all, head_dim)
    shaped_v = value_input.reshape(tok_rows, heads_all, head_dim)
    moved_q, moved_k, moved_v = (
        lax.all_to_all(shaped_q, "seq", split_axis=1, concat_axis=0, tiled=True),
        lax.all_to_all(shaped_k, "seq", split_axis=1, concat_axis=0, tiled=True),
        lax.all_to_all(shaped_v, "seq", split_axis=1, concat_axis=0, tiled=True),
    )
    my_index = lax.axis_index("seq")
    local_heads = lax.dynamic_slice_in_dim(positions, my_index * per_device, per_device)
    local_class = jnp.take(head_class, local_heads)
    local_lists = jnp.take(block_lists, local_heads, axis=0)
    results = []
    first_slot = 0
    for slot_index in range(first_slot, per_device):
        results.append(
            lax.cond(
                local_class[slot_index] == 1,
                dense_head,
                sparse_head,
                moved_q[:, slot_index],
                moved_k[:, slot_index],
                moved_v[:, slot_index],
                local_lists[slot_index],
            )
        )
    mixed = jnp.stack(results, axis=1)
    returned = lax.all_to_all(mixed, "seq", split_axis=0, concat_axis=1, tiled=True)
    return returned.reshape(tok_rows, heads_all * head_dim)


def solution(mesh):
    placed = (
        P(("clip", "seq"), None),
        P(("clip", "seq"), None),
        P(("clip", "seq"), None),
        P("clip"),
        P("clip", None, None),
    )
    return jax.shard_map(
        local, mesh=mesh, in_specs=placed, out_specs=P(("clip", "seq"), None), check_vma=False
    )
```

profile of v0, /device:TPU:1, one launch (start us, length us, event | category | flops | bytes accessed | tf_op | source)
XLA Modules:
  0.0 181.1 jit_solution(14478872423704645470)
XLA Ops:
  0.0 2.4 %copy.68 = bf16[128,4096]{0,1:T(8,128)(2,1)} copy(bf16[128,4096]{1,0:T(8,128)(2,1)} %param.15) | data formatting | bytes 2097152 | tf_op args[0]
  2.4 10.3 %all-to-all-start.1 = ((bf16[128,32,128]{0,2,1:T(8,128)(2,1)}), bf16[128,32,128]{0,2,1:T(8,128)(2,1)S(1)}, u32[]{:S(2)}, u32[]{:S(2)}) async-start(bf16[128,32,128]{0,2,1:T(8,128)(2,1)} %bitcast.38), calls=%async_computation.1 | async-start | bytes 2097152 | tf_op jit(solution)/shard_map/all_to_all | solution.py:75
  12.7 0.0 copy-start.5
  12.8 1.3 copy.64
  14.1 26.7 %all-to-all-done.1 = bf16[128,32,128]{0,2,1:T(8,128)(2,1)S(1)} async-done(((bf16[128,32,128]{0,2,1:T(8,128)(2,1)}), bf16[128,32,128]{0,2,1:T(8,128)(2,1)S(1)}, u32[]{:S(2)}, u32[]{:S(2)}) %all-to-all-start.1) | async-done | bytes 1048608 | tf_op jit(solution)/shard_map/all_to_all | solution.py:75
  40.7 3.6 %all-to-all-start = ((bf16[128,32,128]{0,2,1:T(8,128)(2,1)}), bf16[128,32,128]{0,2,1:T(8,128)(2,1)S(1)}, u32[]{:S(2)}, u32[]{:S(2)}) async-start(bf16[128,32,128]{0,2,1:T(8,128)(2,1)} %bitcast.33), calls=%async_computation | async-start | bytes 2097152 | tf_op jit(solution)/shard_map/all_to_all | solution.py:76
  44.3 1.3 copy.71
  45.6 26.6 %all-to-all-done = bf16[128,32,128]{0,2,1:T(8,128)(2,1)S(1)} async-done(((bf16[128,32,128]{0,2,1:T(8,128)(2,1)}), bf16[128,32,128]{0,2,1:T(8,128)(2,1)S(1)}, u32[]{:S(2)}, u32[]{:S(2)}) %all-to-all-start) | async-done | bytes 1048608 | tf_op jit(solution)/shard_map/all_to_all | solution.py:76
  72.2 3.6 %all-to-all-start.2 = ((bf16[128,32,128]{0,2,1:T(8,128)(2,1)}), bf16[128,32,128]{0,2,1:T(8,128)(2,1)S(1)}, u32[]{:S(2)}, u32[]{:S(2)}) async-start(bf16[128,32,128]{0,2,1:T(8,128)(2,1)} %bitcast.43), calls=%async_computation.2 | async-start | bytes 2097152 | tf_op jit(solution)/shard_map/all_to_all | solution.py:77
  75.7 0.1 compare_and_fusion.2
  75.9 0.6 gather_fusion.4
  76.5 0.6 fusion.69
  78.4 0.1 copy.67
  78.5 0.6 gather_fusion.5
  79.1 0.1 broadcast_select_fusion.4
  79.2 1.3 copy.70
  80.5 1.3 copy.66
  81.8 1.3 fusion.68
  83.1 20.6 %all-to-all-done.2 = bf16[128,32,128]{0,2,1:T(8,128)(2,1)S(1)} async-done(((bf16[128,32,128]{0,2,1:T(8,128)(2,1)}), bf16[128,32,128]{0,2,1:T(8,128)(2,1)S(1)}, u32[]{:S(2)}, u32[]{:S(2)}) %all-to-all-start.2) | async-done | bytes 1048608 | tf_op jit(solution)/shard_map/all_to_all | solution.py:77
  103.6 1.3 copy.73
  104.9 1.7 fusion.66
  106.6 18.9 %conditional.2 = (bf16[2048,1,128]{2,1,0:T(2,128)(2,1)}) conditional(s32[]{:T(128)} %bitcast.32, (bf16[2048,1,128]{2,0,1:T(8,128)(2,1)S(1)}, s32[2,16,4]{1,2,0:T(4,128)S(1)}, bf16[2048,1,128]{2,0,1:T(8,128)(2,1)S(1)}, bf16[2048,1,128]{2,0,1:T(8,128)(2,1)S(1)}) %tuple.30, (bf16[2048,1,128]{2,0,1:T(8,128)(2,1)S(1)}, ...), branch_computations={%region_0.4_spmd, %region_3.9_spmd} | conditional | flops 547878464 | bytes 35699464 | solution.py:87
  106.7 0.1 copy.54
  106.8 0.1 copy.55
  106.8 0.1 reshape.123
  106.9 2.1 %gather_fusion.1 = bf16[64,128,128]{2,1,0:T(8,128)(2,1)} fusion(bf16[16,128,128]{2,1,0:T(8,128)(2,1)S(1)} %bitcast.126, s32[1024]{0:T(1024)S(1)} %pad_clamp_fusion), kind=kCustom, calls=%fused_computation.1.clone | custom fusion | bytes 4194560 | tf_op jit(solution)/shard_map/cond/branch_0_fun/jit(_take)/gather | solution.py:43
  109.1 2.2 %gather_fusion = bf16[64,128,128]{2,1,0:T(8,128)(2,1)} fusion(bf16[16,128,128]{2,1,0:T(8,128)(2,1)S(1)} %bitcast.122, s32[1024]{0:T(1024)S(1)} %pad_clamp_fusion), kind=kCustom, calls=%fused_computation.clone | custom fusion | bytes 4194560 | tf_op jit(solution)/shard_map/cond/branch_0_fun/jit(_take)/gather | solution.py:40
  111.2 2.7 %broadcast_select_fusion.1 = (bf16[16,4,128,128]{3,2,1,0:T(8,128)(2,1)S(1)}, bf16[16,4,128,128]{3,2,1,0:T(8,128)(2,1)S(1)}) fusion(bf16[16,4,128,128]{3,2,1,0:T(8,128)(2,1)} %bitcast.129, pred[16,4]{1,0:T(8,128)(4,1)S(1)} %copy.54, bf16[16,4,128,128]{3,2,1,0:T(8,128)(2,1)} %bitcast.128), kind=kLoop, calls=%fused_computation.47 | loop fusion | flops 2097152 | bytes 8388672 | tf_op jit(solution)/shard_map/cond/branch_0_fun/jit(_take)/select_n | solution.py:40
  113.9 0.7 bitcast_reduce_fusion
  114.6 0.7 fusion.47
  115.3 1.3 divide_convert_fusion
  116.6 8.9 %copy.82 = bf16[2048,1,128]{2,1,0:T(2,128)(2,1)} copy(bf16[2048,1,128]{2,0,1:T(8,128)(2,1)S(1)} %bitcast.149) | data formatting | bytes 1048576 | tf_op jit(solution)/shard_map/cond | solution.py:87
  125.5 17.3 %conditional.3 = (bf16[2048,1,128]{2,1,0:T(2,128)(2,1)S(1)}) conditional(s32[]{:T(128)} %bitcast.48, (bf16[2048,1,128]{2,0,1:T(8,128)(2,1)S(1)}, s32[2,16,4]{1,2,0:T(4,128)S(1)}, bf16[2048,1,128]{2,0,1:T(8,128)(2,1)S(1)}, bf16[2048,1,128]{2,0,1:T(8,128)(2,1)S(1)}) %tuple.32, (bf16[2048,1,128]{2,0,1:T(8,128)(2,1)S(1)}, ...), branch_computations={%region_8.12_spmd, %region_11.17_spmd} | conditional | flops 547878464 | bytes 39893824 | solution.py:87
  125.5 0.1 copy.59
  125.6 0.1 copy.60
  125.7 0.1 reshape.131
  125.8 0.5 copy-done.1
  126.3 0.9 gather_fusion.3
  127.3 2.2 %gather_fusion.2 = bf16[64,128,128]{2,1,0:T(8,128)(2,1)} fusion(bf16[16,128,128]{2,1,0:T(8,128)(2,1)S(1)} %bitcast.120, s32[1024]{0:T(1024)S(1)} %pad_clamp_fusion.1), kind=kCustom, calls=%fused_computation.2.clone | custom fusion | bytes 4194560 | tf_op jit(solution)/shard_map/cond/branch_0_fun/jit(_take)/gather | solution.py:40
  129.5 2.2 %broadcast_select_fusion.3 = (bf16[16,4,128,128]{3,2,1,0:T(8,128)(2,1)S(1)}, bf16[16,4,128,128]{3,2,1,0:T(8,128)(2,1)S(1)}) fusion(bf16[16,4,128,128]{3,2,1,0:T(8,128)(2,1)} %bitcast.131, pred[16,4]{1,0:T(8,128)(4,1)S(1)} %copy.59, bf16[16,4,128,128]{3,2,1,0:T(8,128)(2,1)S(1)} %bitcast.130), kind=kLoop, calls=%fused_computation.62 | loop fusion | flops 2097152 | bytes 8388672 | tf_op jit(solution)/shard_map/cond/branch_0_fun/jit(_take)/select_n | solution.py:40
  131.7 0.7 bitcast_reduce_fusion.1
  132.4 0.7 fusion.57
  133.2 1.3 divide_convert_fusion.1
  134.4 8.1 %copy.84 = bf16[2048,1,128]{2,1,0:T(2,128)(2,1)S(1)} copy(bf16[2048,1,128]{2,0,1:T(8,128)(2,1)S(1)} %bitcast.150) | data formatting | bytes 1048576 | tf_op jit(solution)/shard_map/cond | solution.py:87
  142.8 3.5 %pad_maximum_fusion = bf16[2048,2,128]{2,1,0:T(2,128)(2,1)S(1)} fusion(bf16[2048,1,128]{2,1,0:T(2,128)(2,1)S(1)} %get-tuple-element.127, bf16[2048,1,128]{2,1,0:T(2,128)(2,1)} %get-tuple-element.126), kind=kLoop, calls=%fused_computation.68 | loop fusion | flops 2097152 | bytes 2097152 | tf_op jit(solution)/shard_map/stack | solution.py:97
  146.3 32.5 %all_to_all.69 = bf16[2048,2,128]{2,1,0:T(2,128)(2,1)S(1)} all-to-all(bf16[2048,2,128]{2,1,0:T(2,128)(2,1)S(1)} %pad_maximum_fusion), channel_id=1, replica_groups=mesh['clip'=32,'seq'=16] {'seq'}, dimensions={0} | all-to-all | bytes 2097152 | tf_op jit(solution)/shard_map/all_to_all | solution.py:98
  178.8 0.7 copy.76
  179.5 1.6 reshape.62
  (19 shorter events, 0.1 us)
Async XLA Ops:
  0.0 75.8 %copy-start = (s32[32]{0:T(128)S(1)}, s32[32]{0:T(128)}, u32[]{:S(2)}) copy-start(s32[32]{0:T(128)} %param.18) | copy-start | bytes 388
  0.0 12.7 %copy-start.3 = (bf16[128,4096]{1,0:T(8,128)(2,1)S(1)}, bf16[128,4096]{1,0:T(8,128)(2,1)}, u32[]{:S(2)}) copy-start(bf16[128,4096]{1,0:T(8,128)(2,1)} %param.16) | copy-start | bytes 3145732
  0.0 44.3 %copy-start.4 = (bf16[128,4096]{1,0:T(8,128)(2,1)S(1)}, bf16[128,4096]{1,0:T(8,128)(2,1)}, u32[]{:S(2)}) copy-start(bf16[128,4096]{1,0:T(8,128)(2,1)} %param.17) | copy-start | bytes 3145732
  2.4 38.3 %all-to-all-start.1 = ((bf16[128,32,128]{0,2,1:T(8,128)(2,1)}), bf16[128,32,128]{0,2,1:T(8,128)(2,1)S(1)}, u32[]{:S(2)}, u32[]{:S(2)}) async-start(bf16[128,32,128]{0,2,1:T(8,128)(2,1)} %bitcast.38), calls=%async_computation.1 | async-start | bytes 2097152 | tf_op jit(solution)/shard_map/all_to_all | solution.py:75
  12.7 65.7 %copy-start.5 = (s32[32,16,4]{0,2,1:T(4,128)S(1)}, s32[32,16,4]{0,2,1:T(4,128)}, u32[]{:S(2)}) copy-start(s32[32,16,4]{0,2,1:T(4,128)} %param.19) | copy-start | bytes 24580
  40.7 31.5 %all-to-all-start = ((bf16[128,32,128]{0,2,1:T(8,128)(2,1)}), bf16[128,32,128]{0,2,1:T(8,128)(2,1)S(1)}, u32[]{:S(2)}, u32[]{:S(2)}) async-start(bf16[128,32,128]{0,2,1:T(8,128)(2,1)} %bitcast.33), calls=%async_computation | async-start | bytes 2097152 | tf_op jit(solution)/shard_map/all_to_all | solution.py:76
  72.2 31.5 %all-to-all-start.2 = ((bf16[128,32,128]{0,2,1:T(8,128)(2,1)}), bf16[128,32,128]{0,2,1:T(8,128)(2,1)S(1)}, u32[]{:S(2)}, u32[]{:S(2)}) async-start(bf16[128,32,128]{0,2,1:T(8,128)(2,1)} %bitcast.43), calls=%async_computation.2 | async-start | bytes 2097152 | tf_op jit(solution)/shard_map/all_to_all | solution.py:77
  125.5 0.8 copy-start.1
  129.5 2.3 %copy-start.2 = (bf16[2048,1,128]{2,0,1:T(8,128)(2,1)S(1)}, bf16[2048,1,128]{2,0,1:T(8,128)(2,1)}, u32[]{:S(2)}) copy-start(bf16[2048,1,128]{2,0,1:T(8,128)(2,1)} %copy-done.1) | copy-start | bytes 1572868 | tf_op jit(solution)/shard_map/cond
where the time goes:
time: 182 us; the launch traced here: 181 us
  waiting for transfers between devices  73.8 us (41%)
  local copies, waits for them, and re-layouts  41.7 us (23%)
  blocking collectives  32.5 us (18%)
  starting transfers between devices  17.4 us (10%)
  other arithmetic  9.96 us (5%)
  matrix products  3.95 us (2%)
    all_to_all x1, blocking collectives, local(): lax.all_to_all(mixed, 'seq', split_axis=0, concat_axis=1, tiled=True)  32.5 us
    all_to_all x1, waiting for transfers between devices, local(): lax.all_to_all(shaped_q, 'seq', split_axis=1, concat_axis=0, tiled=True)  26.7 us
    all_to_all x1, waiting for transfers between devices, local(): lax.all_to_all(shaped_k, 'seq', split_axis=1, concat_axis=0, tiled=True)  26.6 us
    all_to_all x1, waiting for transfers between devices, local(): lax.all_to_all(shaped_v, 'seq', split_axis=1, concat_axis=0, tiled=True)  20.6 us
    cond x2, local copies, waits for them, and re-layouts, local(): lax.cond(local_class[slot_index] == 1, dense_head, sparse_head, moved_q[:...  17.1 us
    all_to_all x1, starting transfers between devices, local(): lax.all_to_all(shaped_q, 'seq', split_axis=1, concat_axis=0, tiled=True)  10.3 us
    unnamed x12, local copies, waits for them, and re-layouts  5.15 us
    select_n x4, other arithmetic, sparse_head(): jnp.take(key_head.reshape(block_count, BLOCK_LEN, head_dim), head_lists,...  4.91 us
  transfers between devices with their start and end apart: 3, of which 3 were waited for; matrix products, arithmetic and copies ran while one was open for 5% of the time, Pallas kernels for 0%

commit v1 on v0

v1 whole, which is shorter than its diff:
```python
import functools
import math

import jax
import jax.numpy as jnp
from jax import lax
from jax.experimental import pallas as pl
from jax.experimental.pallas import tpu as pltpu
from jax.sharding import PartitionSpec as P

MESH = pl.DeviceIdType.MESH
BLOCK_LEN = 128


def ring_delta(step, chips):
    return chips // 2 + (1 - 2 * (step % 2)) * ((step + 1) // 2)


def kernel(
    n, per, head_dim, q_ref, k_ref, v_ref, class_ref, lists_ref, out_ref,
    q_buf, k_buf, v_buf, o_buf, bias, class_mem, lists_mem,
    small_sem, send_sem, kv_sem, q_sem, o_send_sem, o_sem,
):
    me = lax.axis_index("seq")
    chips = n // 2
    chip, core = me // 2, me % 2
    rows = q_ref.shape[0]
    tokens = n * rows
    blocks = tokens // BLOCK_LEN

    class_copy = pltpu.make_async_copy(class_ref, class_mem, small_sem.at[0])
    class_copy.start()
    lists_copy = pltpu.make_async_copy(lists_ref, lists_mem, small_sem.at[1])
    lists_copy.start()

    def columns(device, head):
        return pl.ds(pl.multiple_of((device * per + head) * head_dim, head_dim), head_dim)

    def token_rows(device):
        return pl.ds(pl.multiple_of(device * rows, rows), rows)

    def tensors(head, target_row):
        return (
            (k_ref, k_buf, kv_sem.at[head, 0]),
            (v_ref, v_buf, kv_sem.at[head, 1]),
            (q_ref, q_buf, q_sem.at[head, target_row]),
        )

    barrier = pltpu.get_barrier_semaphore()

    def greet(d, carry):
        pl.semaphore_signal(
            barrier, inc=1, device_id={"seq": lax.rem(me + d, n)}, device_id_type=MESH
        )
        return carry

    lax.fori_loop(1, n, greet, 0)

    for head in range(per):
        for src, buf, sem in tensors(head, me):
            pltpu.make_async_copy(
                src.at[:, columns(me, head)], buf.at[head, token_rows(me)], sem
            ).start()

    pl.semaphore_wait(barrier, n - 1)

    def send_inputs(head, which):
        def to_peer(i, carry):
            step = i // 2
            target = lax.rem(chip + ring_delta(step, chips), chips) * 2 + (core + 1 - i % 2) % 2
            for t in which:
                src, buf, sem = tensors(head, me)[t]
                pltpu.make_async_remote_copy(
                    src_ref=src.at[:, columns(target, head)],
                    dst_ref=buf.at[head, token_rows(me)],
                    send_sem=send_sem.at[head, t],
                    recv_sem=sem,
                    device_id={"seq": target},
                    device_id_type=MESH,
                ).start()
            return carry

        lax.fori_loop(0, n - 1, to_peer, 0)

    for head in range(per):
        send_inputs(head, (0, 1))
        send_inputs(head, (2,))

    class_copy.wait()
    lists_copy.wait()
    key_block = lax.broadcasted_iota(jnp.int32, (blocks, tokens), 1) // BLOCK_LEN
    lists = lists_mem[...].astype(jnp.float32)
    head_lane = lax.broadcasted_iota(jnp.int32, (blocks, lists.shape[2]), 1)
    for head in range(per):
        mine = head_lane == me * per + head
        allowed = None
        for j in range(lists.shape[1]):
            listed = jnp.sum(jnp.where(mine, lists[:, j, :], 0.0), axis=1, keepdims=True)
            hit = listed.astype(jnp.int32) == key_block
            allowed = hit if allowed is None else jnp.logical_or(allowed, hit)
        closed = jnp.where(class_mem[me * per + head] == 1, 0.0, -jnp.inf)
        bias[head] = jnp.where(allowed, 0.0, closed)

    factor = math.log2(math.e) / math.sqrt(head_dim)

    for head in range(per):
        pltpu.make_async_copy(k_buf.at[head], k_buf.at[head], kv_sem.at[head, 0]).wait()
        pltpu.make_async_copy(v_buf.at[head], v_buf.at[head], kv_sem.at[head, 1]).wait()

        def attend(step, carry, head=head):
            source_chip = lax.rem(chip + 2 * chips - ring_delta(step, chips), chips)
            for half in range(2):
                device = source_chip * 2 + half
                pltpu.make_async_copy(
                    q_buf.at[head, token_rows(device)],
                    q_buf.at[head, token_rows(device)],
                    q_sem.at[head, device],
                ).wait()
            pair_rows = pl.ds(pl.multiple_of(source_chip * 2 * rows, 2 * rows), 2 * rows)
            scores = lax.dot_general(
                q_buf[head, pair_rows, :],
                k_buf[head],
                (((1,), (1,)), ((), ())),
                preferred_element_type=jnp.float32,
            )
            for half in range(2):
                device = source_chip * 2 + half
                part = scores[half * rows : (half + 1) * rows] + bias[head, pl.ds(device, 1), :]
                largest = jnp.max(part, axis=1, keepdims=True)
                weights = jnp.exp2((part - largest) * factor)
                total = jnp.sum(weights, axis=1, keepdims=True)
                mixed = lax.dot_general(
                    weights.astype(jnp.bfloat16),
                    v_buf[head],
                    (((1,), (0,)), ((), ())),
                    preferred_element_type=jnp.float32,
                )
                o_buf[head, token_rows(device), :] = (mixed / total).astype(jnp.bfloat16)

                @pl.when(device != me)
                def _():
                    pltpu.make_async_remote_copy(
                        src_ref=o_buf.at[head, token_rows(device)],
                        dst_ref=out_ref.at[:, columns(me, head)],
                        send_sem=o_send_sem,
                        recv_sem=o_sem,
                        device_id={"seq": device},
                        device_id_type=MESH,
                    ).start()

                @pl.when(device == me)
                def _():
                    pltpu.make_async_copy(
                        o_buf.at[head, token_rows(device)],
                        out_ref.at[:, columns(me, head)],
                        o_sem,
                    ).start()

            return carry

        lax.fori_loop(0, chips, attend, 0)

    sent = pl.ds(0, (n - 1) * rows)
    for head in range(per):
        for t in range(3):
            pltpu.make_async_copy(
                k_buf.at[head, sent], k_buf.at[head, sent], send_sem.at[head, t]
            ).wait()
    all_sent = o_buf.at[:, sent]
    pltpu.make_async_copy(all_sent, all_sent, o_send_sem).wait()
    pltpu.make_async_copy(out_ref, out_ref, o_sem).wait()


def local(queries, keys_in, value_input, head_class, block_lists):
    n = lax.axis_size("seq")
    rows, width = queries.shape
    heads = head_class.shape[0]
    per = heads // n
    head_dim = width // heads
    tokens = n * rows
    blocks = tokens // BLOCK_LEN
    hbm = pl.BlockSpec(memory_space=pltpu.HBM)
    buffer = pltpu.VMEM((per, tokens, head_dim), jnp.bfloat16)
    return pl.pallas_call(
        functools.partial(kernel, n, per, head_dim),
        out_shape=jax.ShapeDtypeStruct((rows, width), jnp.bfloat16),
        in_specs=[hbm] * 5,
        out_specs=hbm,
        scratch_shapes=[
            buffer,
            buffer,
            buffer,
            buffer,
            pltpu.VMEM((per, blocks, tokens), jnp.float32),
            pltpu.SMEM((heads,), jnp.int32),
            pltpu.VMEM(block_lists.shape[1:] + (heads,), jnp.int32),
            pltpu.SemaphoreType.DMA((2,)),
            pltpu.SemaphoreType.DMA((per, 3)),
            pltpu.SemaphoreType.DMA((per, 2)),
            pltpu.SemaphoreType.DMA((per, n)),
            pltpu.SemaphoreType.DMA,
            pltpu.SemaphoreType.DMA,
        ],
        compiler_params=pltpu.CompilerParams(
            collective_id=0, has_side_effects=True, vmem_limit_bytes=63 << 20
        ),
        cost_estimate=pl.CostEstimate(
            flops=4 * per * tokens * tokens * head_dim,
            bytes_accessed=8 * rows * width,
            transcendentals=per * tokens * tokens,
        ),
    )(queries, keys_in, value_input, head_class, jnp.transpose(block_lists, (1, 2, 0)))


def solution(mesh):
    placed = (
        P(("clip", "seq"), None),
        P(("clip", "seq"), None),
        P(("clip", "seq"), None),
        P("clip"),
        P("clip", None, None),
    )
    return jax.shard_map(
        local, mesh=mesh, in_specs=placed, out_specs=P(("clip", "seq"), None), check_vma=False
    )
```

time: 182 us -> 104 us (0.57)
  Pallas kernels: 0 us -> 102 us
  waiting for transfers between devices: 73.8 us -> 0 us
  local copies, waits for them, and re-layouts: 41.7 us -> 2.29 us
  blocking collectives: 32.5 us -> 0 us
  starting transfers between devices: 17.4 us -> 0 us
  other arithmetic: 9.96 us -> 0 us
  matrix products: 3.95 us -> 0 us
    pallas_call x0 -> x1, Pallas kernels: none -> 102 us  [local(): pl.pallas_call(functools.partial(kernel, n, per, head_dim), out_shape=jax...]
    all_to_all x3 -> x0, waiting for transfers between devices: 73.8 us -> none  [the longest x1 26.7 us: local(): lax.all_to_all(shaped_q, 'seq', split_axis=1, concat_axis=0, tiled=True)]
    all_to_all x1 -> x0, blocking collectives: 32.5 us -> none  [local(): lax.all_to_all(mixed, 'seq', split_axis=0, concat_axis=1, tiled=True)]
    cond x6 -> x0, local copies, waits for them, and re-layouts: 17.6 us -> none  [the longest x2 17.1 us: local(): lax.cond(local_class[slot_index] == 1, dense_head, sparse_head, moved_q[:...]
    all_to_all x3 -> x0, starting transfers between devices: 17.4 us -> none  [the longest x1 10.3 us: local(): lax.all_to_all(shaped_q, 'seq', split_axis=1, concat_axis=0, tiled=True)]
    gather x6 -> x0, local copies, waits for them, and re-layouts: 8.63 us -> none  [the longest x2 4.34 us: sparse_head(): jnp.take(key_head.reshape(block_count, BLOCK_LEN, head_dim), head_lists,...]
    select_n x6 -> x0, other arithmetic: 4.99 us -> none  [the longest x4 4.91 us: sparse_head(): jnp.take(key_head.reshape(block_count, BLOCK_LEN, head_dim), head_lists,...]
    all_to_all x4 -> x0, local copies, waits for them, and re-layouts: 4.66 us -> none  [the longest x1 1.33 us: local(): lax.all_to_all(shaped_q, 'seq', split_axis=1, concat_axis=0, tiled=True)]
  transfers between devices with their start and end apart: 3 -> 0, of which waited for: 3 -> 0; matrix products, arithmetic and copies ran while one was open for 5% -> 0% of each run, Pallas kernels for 0% -> 0%
where the time goes in v1:
time: 104 us
  Pallas kernels  102 us (98%)
  local copies, waits for them, and re-layouts  2.29 us (2%)
    pallas_call x1, Pallas kernels, local(): pl.pallas_call(functools.partial(kernel, n, per, head_dim), out_shape=jax...  102 us
    unnamed x1, local copies, waits for them, and re-layouts  2.29 us

profile of v1, /device:TPU:1, one launch (start us, length us, event | category | flops | bytes accessed | tf_op | source)
XLA Modules:
  0.0 104.3 jit_solution(7262589887003118481)
XLA Ops:
  0.0 102.0 %shard_map.55 = bf16[128,4096]{1,0:T(8,128)(2,1)} custom-call(bf16[128,4096]{1,0:T(8,128)(2,1)} %q_ref.1, bf16[128,4096]{1,0:T(8,128)(2,1)} %k_ref.1, bf16[128,4096]{1,0:T(8,128)(2,1)} %v_ref.1, s32[32]{0:T(128)} %class_ref.1, s32[16,4,32]{2,1,0:T(4,128)} %bitcast.1), custom_call_target="tpu_custom_call" | custom-call | flops 4294967296 | bytes 4194304 | tf_op jit(solution)/shard_map/pallas_call | solution.py:184
  102.0 2.3 %copy.7 = bf16[128,4096]{1,0:T(8,128)(2,1)} copy(bf16[128,4096]{1,0:T(8,128)(2,1)} %shard_map.55) | data formatting | bytes 2097152

commit v2 on v1

--- a/solution.py
+++ b/solution.py
@@ -13,7 +13,7 @@
 
 
 def ring_delta(step, chips):
-    return chips // 2 + (1 - 2 * (step % 2)) * ((step + 1) // 2)
+    return (1 - 2 * (step % 2)) * ((step + 1) // 2) + (step==chips-1)*0
 
 
 def kernel(
@@ -67,7 +67,7 @@
     def send_inputs(head, which):
         def to_peer(i, carry):
             step = i // 2
-            target = lax.rem(chip + ring_delta(step, chips), chips) * 2 + (core + 1 - i % 2) % 2
+            target = lax.rem(chip + chips + ring_delta((i+1)//2, chips), chips) * 2 + (core + (i+1) % 2) % 2
             for t in which:
                 src, buf, sem = tensors(head, me)[t]
                 pltpu.make_async_remote_copy(
@@ -183,9 +183,9 @@
     buffer = pltpu.VMEM((per, tokens, head_dim), jnp.bfloat16)
     return pl.pallas_call(
         functools.partial(kernel, n, per, head_dim),
-        out_shape=jax.ShapeDtypeStruct((rows, width), jnp.bfloat16),
+        out_shape=pltpu.VMEM((rows, width), jnp.bfloat16),
         in_specs=[hbm] * 5,
-        out_specs=hbm,
+        out_specs=pl.BlockSpec(memory_space=pltpu.VMEM),
         scratch_shapes=[
             buffer,
             buffer,
@@ -202,14 +202,19 @@
             pltpu.SemaphoreType.DMA,
         ],
         compiler_params=pltpu.CompilerParams(
-            collective_id=0, has_side_effects=True, vmem_limit_bytes=63 << 20
+            collective_id=0, has_side_effects=True, vmem_limit_bytes=48 << 20
         ),
         cost_estimate=pl.CostEstimate(
             flops=4 * per * tokens * tokens * head_dim,
             bytes_accessed=8 * rows * width,
             transcendentals=per * tokens * tokens,
         ),
-    )(queries, keys_in, value_input, head_class, jnp.transpose(block_lists, (1, 2, 0)))
+    )(
+        *(
+            pltpu.with_memory_space_constraint(x, pltpu.HBM)
+            for x in (queries, keys_in, value_input, head_class, jnp.transpose(block_lists, (1, 2, 0)))
+        )
+    )
 
 
 def solution(mesh):

time: 104 us -> 104 us (level)
  local copies, waits for them, and re-layouts: 2.29 us -> 0.97 us
    unnamed x1, local copies, waits for them, and re-layouts: 2.29 us -> 0.97 us
where the time goes in v2:
time: 104 us
  Pallas kernels  103 us (99%)
    pallas_call x1, Pallas kernels, local(): pl.pallas_call(functools.partial(kernel, n, per, head_dim), out_shape=plt...  103 us

profile of v2, /device:TPU:1, one launch (start us, length us, event | category | flops | bytes accessed | tf_op | source)
XLA Modules:
  0.0 103.5 jit_solution(11483784602222298994)
XLA Ops:
  0.0 102.6 %shard_map.55 = bf16[128,4096]{1,0:T(8,128)(2,1)S(1)} custom-call(bf16[128,4096]{1,0:T(8,128)(2,1)} %q_ref.1, bf16[128,4096]{1,0:T(8,128)(2,1)} %k_ref.1, bf16[128,4096]{1,0:T(8,128)(2,1)} %v_ref.1, s32[32]{0:T(128)} %class_ref.1, s32[16,4,32]{2,1,0:T(4,128)} %bitcast.1), custom_call_target="tpu_custom_call" | custom-call | flops 4294967296 | bytes 4194304 | tf_op jit(solution)/shard_map/pallas_call | solution.py:184
  102.6 1.0 copy.7

commit v3 on v2

--- a/solution.py
+++ b/solution.py
@@ -12,14 +12,14 @@
 BLOCK_LEN = 128
 
 
-def ring_delta(step, chips):
-    return (1 - 2 * (step % 2)) * ((step + 1) // 2) + (step==chips-1)*0
+def ring_delta(step):
+    return (2 * (step % 2) - 1) * ((step + 1) // 2)
 
 
 def kernel(
     n, per, head_dim, q_ref, k_ref, v_ref, class_ref, lists_ref, out_ref,
     q_buf, k_buf, v_buf, o_buf, bias, class_mem, lists_mem,
-    small_sem, send_sem, kv_sem, q_sem, o_send_sem, o_sem,
+    late_sem, small_sem, send_sem, kv_sem, q_sem, o_send_sem, o_sem,
 ):
     me = lax.axis_index("seq")
     chips = n // 2
@@ -47,14 +47,21 @@
         )
 
     barrier = pltpu.get_barrier_semaphore()
+    has_late = lax.axis_index("clip") == 0
+    is_late = jnp.logical_and(has_late, me == 0)
+
+    def others(d):
+        return lax.rem(me + d, n)
 
     def greet(d, carry):
         pl.semaphore_signal(
-            barrier, inc=1, device_id={"seq": lax.rem(me + d, n)}, device_id_type=MESH
-        )
-        return carry
-
-    lax.fori_loop(1, n, greet, 0)
+            barrier, inc=1, device_id={"seq": others(d)}, device_id_type=MESH
+        )
+        return carry
+
+    @pl.when(jnp.logical_not(is_late))
+    def _():
+        lax.fori_loop(1, n, greet, 0)
 
     for head in range(per):
         for src, buf, sem in tensors(head, me):
@@ -62,29 +69,57 @@
                 src.at[:, columns(me, head)], buf.at[head, token_rows(me)], sem
             ).start()
 
-    pl.semaphore_wait(barrier, n - 1)
-
-    def send_inputs(head, which):
-        def to_peer(i, carry):
-            step = i // 2
-            target = lax.rem(chip + chips + ring_delta((i+1)//2, chips), chips) * 2 + (core + (i+1) % 2) % 2
-            for t in which:
-                src, buf, sem = tensors(head, me)[t]
-                pltpu.make_async_remote_copy(
-                    src_ref=src.at[:, columns(target, head)],
-                    dst_ref=buf.at[head, token_rows(me)],
-                    send_sem=send_sem.at[head, t],
-                    recv_sem=sem,
-                    device_id={"seq": target},
-                    device_id_type=MESH,
-                ).start()
-            return carry
-
-        lax.fori_loop(0, n - 1, to_peer, 0)
-
-    for head in range(per):
-        send_inputs(head, (0, 1))
-        send_inputs(head, (2,))
+    pl.semaphore_wait(
+        barrier, jnp.where(jnp.logical_and(has_late, me > 0), n - 2, n - 1)
+    )
+
+    def answer(d, carry):
+        pl.semaphore_signal(
+            late_sem, inc=1, device_id={"seq": others(d)}, device_id_type=MESH
+        )
+        return carry
+
+    @pl.when(is_late)
+    def _():
+        lax.fori_loop(1, n, answer, 0)
+
+    def peer(i):
+        target_chip = lax.rem(chip + chips + ring_delta((i + 1) // 2), chips)
+        return target_chip * 2 + (core + (i + 1) % 2) % 2
+
+    def send(target, head):
+        for t, (src, buf, sem) in enumerate(tensors(head, me)):
+            pltpu.make_async_remote_copy(
+                src_ref=src.at[:, columns(target, head)],
+                dst_ref=buf.at[head, token_rows(me)],
+                send_sem=send_sem.at[head, t],
+                recv_sem=sem,
+                device_id={"seq": target},
+                device_id_type=MESH,
+            ).start()
+
+    def first_head(i, carry):
+        target = peer(i)
+
+        @pl.when(jnp.logical_not(jnp.logical_and(has_late, target == 0)))
+        def _():
+            send(target, 0)
+
+        return carry
+
+    lax.fori_loop(0, n - 1, first_head, 0)
+
+    @pl.when(jnp.logical_and(has_late, me > 0))
+    def _():
+        pl.semaphore_wait(late_sem, 1)
+        send(0, 0)
+
+    def later_head(i, carry, head):
+        send(peer(i), head)
+        return carry
+
+    for head in range(1, per):
+        lax.fori_loop(0, n - 1, functools.partial(later_head, head=head), 0)
 
     class_copy.wait()
     lists_copy.wait()
@@ -108,7 +143,7 @@
         pltpu.make_async_copy(v_buf.at[head], v_buf.at[head], kv_sem.at[head, 1]).wait()
 
         def attend(step, carry, head=head):
-            source_chip = lax.rem(chip + 2 * chips - ring_delta(step, chips), chips)
+            source_chip = lax.rem(chip + chips - ring_delta(step), chips)
             for half in range(2):
                 device = source_chip * 2 + half
                 pltpu.make_async_copy(
@@ -194,6 +229,7 @@
             pltpu.VMEM((per, blocks, tokens), jnp.float32),
             pltpu.SMEM((heads,), jnp.int32),
             pltpu.VMEM(block_lists.shape[1:] + (heads,), jnp.int32),
+            pltpu.SemaphoreType.REGULAR,
             pltpu.SemaphoreType.DMA((2,)),
             pltpu.SemaphoreType.DMA((per, 3)),
             pltpu.SemaphoreType.DMA((per, 2)),

time: 104 us -> 99.6 us (0.958)
  Pallas kernels: 103 us -> 97.6 us
    pallas_call x1, Pallas kernels: 103 us -> 97.6 us  [local(): pl.pallas_call(functools.partial(kernel, n, per, head_dim), out_shape=plt...]
where the time goes in v3:
time: 99.6 us; the launch traced here: 98.5 us
  Pallas kernels  97.6 us (98%)
    pallas_call x1, Pallas kernels, local(): pl.pallas_call(functools.partial(kernel, n, per, head_dim), out_shape=plt...  97.6 us

profile of v3, /device:TPU:1, one launch (start us, length us, event | category | flops | bytes accessed | tf_op | source)
XLA Modules:
  0.0 98.5 jit_solution(15690416018354656859)
XLA Ops:
  0.0 97.6 %shard_map.55 = bf16[128,4096]{1,0:T(8,128)(2,1)S(1)} custom-call(bf16[128,4096]{1,0:T(8,128)(2,1)} %q_ref.1, bf16[128,4096]{1,0:T(8,128)(2,1)} %k_ref.1, bf16[128,4096]{1,0:T(8,128)(2,1)} %v_ref.1, s32[32]{0:T(128)} %class_ref.1, s32[16,4,32]{2,1,0:T(4,128)} %bitcast.1), custom_call_target="tpu_custom_call" | custom-call | flops 4294967296 | bytes 4194304 | tf_op jit(solution)/shard_map/pallas_call | solution.py:219
  97.6 1.0 copy.7

commit v4 on v3

--- a/solution.py
+++ b/solution.py
@@ -16,10 +16,21 @@
     return (2 * (step % 2) - 1) * ((step + 1) // 2)
 
 
+def early_first(chip, step, early, chips):
+    out = step
+    seen = early
+    for k in range(chips):
+        other = lax.rem(chip + 2 * chips - ring_delta(chips - 1 - k), chips)
+        is_new = other >= early
+        out = jnp.where(jnp.logical_and(is_new, step == seen), other, out)
+        seen = seen + is_new.astype(jnp.int32)
+    return out
+
+
 def kernel(
     n, per, head_dim, q_ref, k_ref, v_ref, class_ref, lists_ref, out_ref,
     q_buf, k_buf, v_buf, o_buf, bias, class_mem, lists_mem,
-    late_sem, small_sem, send_sem, kv_sem, q_sem, o_send_sem, o_sem,
+    late_sem, wave_sem, small_sem, send_sem, kv_sem, q_sem, o_send_sem, o_sem,
 ):
     me = lax.axis_index("seq")
     chips = n // 2
@@ -28,11 +39,6 @@
     tokens = n * rows
     blocks = tokens // BLOCK_LEN
 
-    class_copy = pltpu.make_async_copy(class_ref, class_mem, small_sem.at[0])
-    class_copy.start()
-    lists_copy = pltpu.make_async_copy(lists_ref, lists_mem, small_sem.at[1])
-    lists_copy.start()
-
     def columns(device, head):
         return pl.ds(pl.multiple_of((device * per + head) * head_dim, head_dim), head_dim)
 
@@ -49,19 +55,29 @@
     barrier = pltpu.get_barrier_semaphore()
     has_late = lax.axis_index("clip") == 0
     is_late = jnp.logical_and(has_late, me == 0)
-
-    def others(d):
-        return lax.rem(me + d, n)
-
-    def greet(d, carry):
-        pl.semaphore_signal(
-            barrier, inc=1, device_id={"seq": others(d)}, device_id_type=MESH
-        )
-        return carry
-
-    @pl.when(jnp.logical_not(is_late))
-    def _():
-        lax.fori_loop(1, n, greet, 0)
+    on_time = jnp.logical_not(is_late)
+
+    def at(distance, which):
+        return lax.rem(chip + chips + distance, chips) * 2 + which
+
+    def signal(sem, target):
+        pl.semaphore_signal(sem, inc=1, device_id={"seq": target}, device_id_type=MESH)
+
+    near = (at(0, 1 - core), at(1, 0), at(1, 1), at(-1, 0), at(-1, 1))
+
+    @pl.when(on_time)
+    def _():
+        for target in near:
+            signal(barrier, target)
+
+    @pl.when(jnp.logical_and(has_late, jnp.logical_and(chip > 1, chip < chips - 1)))
+    def _():
+        signal(barrier, 0)
+
+    class_copy = pltpu.make_async_copy(class_ref, class_mem, small_sem.at[0])
+    class_copy.start()
+    lists_copy = pltpu.make_async_copy(lists_ref, lists_mem, small_sem.at[1])
+    lists_copy.start()
 
     for head in range(per):
         for src, buf, sem in tensors(head, me):
@@ -69,23 +85,29 @@
                 src.at[:, columns(me, head)], buf.at[head, token_rows(me)], sem
             ).start()
 
-    pl.semaphore_wait(
-        barrier, jnp.where(jnp.logical_and(has_late, me > 0), n - 2, n - 1)
-    )
+    beside_late = jnp.logical_and(has_late, jnp.logical_or(chip <= 1, chip == chips - 1))
+    few = jnp.where(beside_late, len(near) - 1, len(near))
+    pl.semaphore_wait(barrier, jnp.where(is_late, n - 1, few))
 
     def answer(d, carry):
-        pl.semaphore_signal(
-            late_sem, inc=1, device_id={"seq": others(d)}, device_id_type=MESH
-        )
+        signal(late_sem, lax.rem(me + d, n))
         return carry
 
     @pl.when(is_late)
     def _():
         lax.fori_loop(1, n, answer, 0)
 
-    def peer(i):
-        target_chip = lax.rem(chip + chips + ring_delta((i + 1) // 2), chips)
-        return target_chip * 2 + (core + (i + 1) % 2) % 2
+    def unless_late(target, act):
+        pl.when(jnp.logical_not(jnp.logical_and(has_late, target == 0)))(act)
+
+    def tell(side, wave):
+        for which in range(2):
+            target = at(side, which)
+            unless_late(target, lambda: signal(wave_sem.at[(1 - side) // 2, wave - 2], target))
+
+    def hear(side, wave):
+        told = jnp.where(jnp.logical_and(has_late, at(side, 0) == 0), 1, 2)
+        pl.semaphore_wait(wave_sem.at[(1 + side) // 2, wave - 2], told)
 
     def send(target, head):
         for t, (src, buf, sem) in enumerate(tensors(head, me)):
@@ -98,21 +120,45 @@
                 device_id_type=MESH,
             ).start()
 
-    def first_head(i, carry):
-        target = peer(i)
-
-        @pl.when(jnp.logical_not(jnp.logical_and(has_late, target == 0)))
+    def send_first(distance):
+        def one(which, carry):
+            target = at(distance, which)
+            unless_late(target, lambda: send(target, 0))
+            return carry
+
+        lax.fori_loop(0, 2, one, 0)
+
+    @pl.when(on_time)
+    def _():
+        tell(-1, 2)
+        tell(1, 2)
+
+    unless_late(near[0], lambda: send(near[0], 0))
+    send_first(1)
+    send_first(-1)
+    for wave in range(2, chips // 2 + 1):
+
+        @pl.when(on_time)
         def _():
-            send(target, 0)
-
-        return carry
-
-    lax.fori_loop(0, n - 1, first_head, 0)
+            hear(1, wave)
+            if wave < chips // 2:
+                tell(-1, wave + 1)
+                hear(-1, wave)
+            if wave + 1 < chips // 2:
+                tell(1, wave + 1)
+
+        send_first(wave)
+        if wave < chips // 2:
+            send_first(-wave)
 
     @pl.when(jnp.logical_and(has_late, me > 0))
     def _():
         pl.semaphore_wait(late_sem, 1)
         send(0, 0)
+
+    def peer(i):
+        target_chip = lax.rem(chip + chips + ring_delta((i + 1) // 2), chips)
+        return target_chip * 2 + (core + (i + 1) % 2) % 2
 
     def later_head(i, carry, head):
         send(peer(i), head)
@@ -143,7 +189,7 @@
         pltpu.make_async_copy(v_buf.at[head], v_buf.at[head], kv_sem.at[head, 1]).wait()
 
         def attend(step, carry, head=head):
-            source_chip = lax.rem(chip + chips - ring_delta(step), chips)
+            source_chip = early_first(chip, step, 2, chips)
             for half in range(2):
                 device = source_chip * 2 + half
                 pltpu.make_async_copy(
@@ -230,6 +276,7 @@
             pltpu.SMEM((heads,), jnp.int32),
             pltpu.VMEM(block_lists.shape[1:] + (heads,), jnp.int32),
             pltpu.SemaphoreType.REGULAR,
+            pltpu.SemaphoreType.REGULAR((2, n // 4 - 1)),
             pltpu.SemaphoreType.DMA((2,)),
             pltpu.SemaphoreType.DMA((per, 3)),
             pltpu.SemaphoreType.DMA((per, 2)),

time: 99.6 us -> 98.2 us (0.986)
  no operation moved by 1% of the time
where the time goes in v4:
time: 98.2 us; the launch traced here: 98.1 us
  Pallas kernels  97.1 us (99%)
    pallas_call x1, Pallas kernels, local(): pl.pallas_call(functools.partial(kernel, n, per, head_dim), out_shape=plt...  97.1 us

profile of v4, /device:TPU:1, one launch (start us, length us, event | category | flops | bytes accessed | tf_op | source)
XLA Modules:
  0.0 98.1 jit_solution(10348904728073939640)
XLA Ops:
  0.0 97.1 %shard_map.55 = bf16[128,4096]{1,0:T(8,128)(2,1)S(1)} custom-call(bf16[128,4096]{1,0:T(8,128)(2,1)} %q_ref.1, bf16[128,4096]{1,0:T(8,128)(2,1)} %k_ref.1, bf16[128,4096]{1,0:T(8,128)(2,1)} %v_ref.1, s32[32]{0:T(128)} %class_ref.1, s32[16,4,32]{2,1,0:T(4,128)} %bitcast.1), custom_call_target="tpu_custom_call" | custom-call | flops 4294967296 | bytes 4194304 | tf_op jit(solution)/shard_map/pallas_call | solution.py:265
  97.1 1.0 copy.7

commit v5 on v4

--- a/solution.py
+++ b/solution.py
@@ -10,20 +10,25 @@
 
 MESH = pl.DeviceIdType.MESH
 BLOCK_LEN = 128
+EARLY = (0,)
 
 
 def ring_delta(step):
     return (2 * (step % 2) - 1) * ((step + 1) // 2)
 
 
-def early_first(chip, step, early, chips):
-    out = step
-    seen = early
+def service(chip, step, chips):
+    out = EARLY[0]
+    for k in range(1, len(EARLY)):
+        out = jnp.where(step == k, EARLY[k], out)
+    seen = len(EARLY)
     for k in range(chips):
         other = lax.rem(chip + 2 * chips - ring_delta(chips - 1 - k), chips)
-        is_new = other >= early
-        out = jnp.where(jnp.logical_and(is_new, step == seen), other, out)
-        seen = seen + is_new.astype(jnp.int32)
+        fresh = other >= 0
+        for e in EARLY:
+            fresh = jnp.logical_and(fresh, other != e)
+        out = jnp.where(jnp.logical_and(fresh, step == seen), other, out)
+        seen = seen + fresh.astype(jnp.int32)
     return out
 
 
@@ -189,7 +194,7 @@
         pltpu.make_async_copy(v_buf.at[head], v_buf.at[head], kv_sem.at[head, 1]).wait()
 
         def attend(step, carry, head=head):
-            source_chip = early_first(chip, step, 2, chips)
+            source_chip = service(chip, step, chips)
             for half in range(2):
                 device = source_chip * 2 + half
                 pltpu.make_async_copy(
@@ -204,7 +209,7 @@
                 (((1,), (1,)), ((), ())),
                 preferred_element_type=jnp.float32,
             )
-            for half in range(2):
+            for half in (1, 0):
                 device = source_chip * 2 + half
                 part = scores[half * rows : (half + 1) * rows] + bias[head, pl.ds(device, 1), :]
                 largest = jnp.max(part, axis=1, keepdims=True)

time: 98.2 us -> 98.1 us (level); the launches traced: 98.1 us -> 97 us
  Pallas kernels: 97.1 us -> 96 us
    pallas_call x1, Pallas kernels: 97.1 us -> 96 us  [local(): pl.pallas_call(functools.partial(kernel, n, per, head_dim), out_shape=plt...]
where the time goes in v5:
time: 98.1 us; the launch traced here: 97 us
  Pallas kernels  96 us (98%)
    pallas_call x1, Pallas kernels, local(): pl.pallas_call(functools.partial(kernel, n, per, head_dim), out_shape=plt...  96 us

profile of v5, /device:TPU:1, one launch (start us, length us, event | category | flops | bytes accessed | tf_op | source)
XLA Modules:
  0.0 97.0 jit_solution(635619797630786805)
XLA Ops:
  0.0 96.0 %shard_map.55 = bf16[128,4096]{1,0:T(8,128)(2,1)S(1)} custom-call(bf16[128,4096]{1,0:T(8,128)(2,1)} %q_ref.1, bf16[128,4096]{1,0:T(8,128)(2,1)} %k_ref.1, bf16[128,4096]{1,0:T(8,128)(2,1)} %v_ref.1, s32[32]{0:T(128)} %class_ref.1, s32[16,4,32]{2,1,0:T(4,128)} %bitcast.1), custom_call_target="tpu_custom_call" | custom-call | flops 4294967296 | bytes 4194304 | tf_op jit(solution)/shard_map/pallas_call | solution.py:270
  96.0 1.0 %copy.7 = bf16[128,4096]{1,0:T(8,128)(2,1)} copy(bf16[128,4096]{1,0:T(8,128)(2,1)S(1)} %shard_map.55) | data formatting | bytes 2097152

commit v6 on v5

--- a/solution.py
+++ b/solution.py
@@ -209,7 +209,7 @@
                 (((1,), (1,)), ((), ())),
                 preferred_element_type=jnp.float32,
             )
-            for half in (1, 0):
+            for half in (1, 0) if head % 2 else (0, 1):
                 device = source_chip * 2 + half
                 part = scores[half * rows : (half + 1) * rows] + bias[head, pl.ds(device, 1), :]
                 largest = jnp.max(part, axis=1, keepdims=True)

time: 98.1 us -> 98.1 us (level)
  no operation moved by 1% of the time
where the time goes in v6:
time: 98.1 us; the launch traced here: 97 us
  Pallas kernels  96 us (98%)
    pallas_call x1, Pallas kernels, local(): pl.pallas_call(functools.partial(kernel, n, per, head_dim), out_shape=plt...  96 us

profile of v6, /device:TPU:1, one launch (start us, length us, event | category | flops | bytes accessed | tf_op | source)
XLA Modules:
  0.0 97.0 jit_solution(17313006506002423451)
XLA Ops:
  0.0 96.0 %shard_map.55 = bf16[128,4096]{1,0:T(8,128)(2,1)S(1)} custom-call(bf16[128,4096]{1,0:T(8,128)(2,1)} %q_ref.1, bf16[128,4096]{1,0:T(8,128)(2,1)} %k_ref.1, bf16[128,4096]{1,0:T(8,128)(2,1)} %v_ref.1, s32[32]{0:T(128)} %class_ref.1, s32[16,4,32]{2,1,0:T(4,128)} %bitcast.1), custom_call_target="tpu_custom_call" | custom-call | flops 4294967296 | bytes 4194304 | tf_op jit(solution)/shard_map/pallas_call | solution.py:270
  96.0 1.0 %copy.7 = bf16[128,4096]{1,0:T(8,128)(2,1)} copy(bf16[128,4096]{1,0:T(8,128)(2,1)S(1)} %shard_map.55) | data formatting | bytes 2097152

commit v7 on v6

--- a/solution.py
+++ b/solution.py
@@ -194,7 +194,7 @@
         pltpu.make_async_copy(v_buf.at[head], v_buf.at[head], kv_sem.at[head, 1]).wait()
 
         def attend(step, carry, head=head):
-            source_chip = service(chip, step, chips)
+            source_chip = service(chip, step, chips) if head else lax.rem(chip + chips - ring_delta(step), chips)
             for half in range(2):
                 device = source_chip * 2 + half
                 pltpu.make_async_copy(

time: 98.1 us -> 98.1 us (level)
  the two profiles are of different devices: /device:TPU:1 before, /device:TPU:8 now
where the time goes in v7:
time: 98.1 us; the launch traced here: 98 us
  Pallas kernels  97 us (99%)
    pallas_call x1, Pallas kernels, local(): pl.pallas_call(functools.partial(kernel, n, per, head_dim), out_shape=plt...  97 us

profile of v7, /device:TPU:8, one launch (start us, length us, event | category | flops | bytes accessed | tf_op | source)
XLA Modules:
  0.0 98.0 jit_solution(4267775243531736011)
XLA Ops:
  0.0 97.0 %shard_map.55 = bf16[128,4096]{1,0:T(8,128)(2,1)S(1)} custom-call(bf16[128,4096]{1,0:T(8,128)(2,1)} %q_ref.1, bf16[128,4096]{1,0:T(8,128)(2,1)} %k_ref.1, bf16[128,4096]{1,0:T(8,128)(2,1)} %v_ref.1, s32[32]{0:T(128)} %class_ref.1, s32[16,4,32]{2,1,0:T(4,128)} %bitcast.1), custom_call_target="tpu_custom_call" | custom-call | flops 4294967296 | bytes 4194304 | tf_op jit(solution)/shard_map/pallas_call | solution.py:270
  97.0 1.0 copy.7
